TPU v7x, 32 devices: a whole 2x2x4 slice. The times are simulated.
32 devices in a mesh: req: 8 (over y, x, core), kv: 4 (over z).
Axes of the slice: x: 2, y: 2, z: 4, core: 2. Of those that a mesh axis runs over, the one named last changes fastest.
Arguments:
- hidden_in: bfloat16 [512, 5120], P('req'), may hold values from -6 to 6
- norm_gain: bfloat16 [5120], replicated, may hold values from 0.25 to 1.75
- w_query: bfloat16 [5120, 5120], P(None, 'kv'), may hold values from -1 to 1
- key_projection: bfloat16 [5120, 1024], P(None, 'kv'), may hold values from -4 to 4
- value_projection: bfloat16 [5120, 1024], P(None, 'kv'), may hold values from -0.15625 to 0.15625
- w_out: bfloat16 [5120, 5120], P('kv'), may hold values from -0.3125 to 0.3125
- pre_keys: bfloat16 [48, 2048, 1024], P('req', None, 'kv'), may hold values from -360 to 360
- prompt_values: bfloat16 [48, 2048, 1024], P('req', None, 'kv'), may hold values from -18 to 18
- continuation_keys: bfloat16 [512, 64, 1024], P('req', None, 'kv'), may hold values from -12 to 12
- continuation_values: bfloat16 [512, 64, 1024], P('req', None, 'kv'), may hold values from -18 to 18
- group_seq: int32 [512], replicated, may hold values from 0 to 47, never falling along the last dimension, each value on 1 to 16 neighbouring positions
- request_order: int32 [512], replicated, may hold values from 0 to 511, each once
- pre_len: int32 [48], replicated, may hold values from 1 to 2048, 73728 in all
- continuation_length: int32 [512], P('req'), may hold values from 1 to 64, 16384 in all
Outputs:
- attn_out: bfloat16 [512, 5120], P('req', 'kv')
Inputs may be any that keep to these rules, and one draw needn't show every extreme that they name: `group_seq`: group numbers never fall along the list; each group holds 1 to 16 requests, and some group exactly 16. `request_order`: each request once. `pre_len`: some group has exactly 2048. `continuation_length`: some request has exactly 64.
All inputs are finite; a program needn't handle non-finite values. No bound on the sum of `continuation_length` on one device may be relied on, other than what follows from the above.
Results may differ from a plain program's by a relative error of at most 0.012.
The roundings to bfloat16 on the way count: a program that leaves them out, or rounds other values in their place, can miss the bound.
Values may be sent and summed in bfloat16 or wider, within the bound.
A program may use at most 192 MiB of HBM per device.

v0:
```python
import math

import jax
import jax.numpy as jnp
from jax import lax
from jax.sharding import PartitionSpec as P

QUERY_HEADS = 40
KEY_VALUE_HEADS = 8
HEAD_SIZE = 128
GROUP_CAPACITY = 16


EPS = 1e-06
THETA = 1000000.0


def apply_rotary(value_rows, token_position):
    half = value_rows.shape[-1] // 2
    freq = jnp.exp(
        -math.log(THETA) * 2.0 * jnp.arange(half, dtype=jnp.float32) / value_rows.shape[-1]
    )
    angle = token_position.astype(jnp.float32)[:, None] * freq[None, :]
    cosine = jnp.cos(angle)[:, None, :]
    sine = jnp.sin(angle)[:, None, :]
    leading_index = value_rows[..., :half]
    second = value_rows[..., half:]
    return jnp.concatenate(
        [leading_index * cosine - second * sine, second * cosine + leading_index * sine], axis=-1
    )


def continuation_partial(query_vector, fresh_key, fresh_value, key_rows, value_rows, live_length):
    scale = 1.0 / math.sqrt(query_vector.shape[-1])
    scores = (
        jnp.einsum("rkgd,rtkd->rkgt", query_vector, key_rows, preferred_element_type=jnp.float32)
        * scale
    )
    live = (
        jnp.arange(key_rows.shape[1], dtype=jnp.int32)[None, None, None, :]
        < live_length[:, None, None, None]
    )
    scores = jnp.where(live, scores, -jnp.inf)
    own = (
        jnp.einsum("rkgd,rkd->rkg", query_vector, fresh_key, preferred_element_type=jnp.float32)
        * scale
    )
    top = jnp.maximum(jnp.max(scores, axis=-1), own)
    weights = jnp.where(live, jnp.exp(scores - top[..., None]), 0.0)
    own_weight = jnp.exp(own - top)
    total = jnp.sum(weights, axis=-1) + own_weight
    numer = jnp.einsum(
        "rkgt,rtkd->rkgd",
        weights.astype(jnp.bfloat16),
        value_rows,
        preferred_element_type=jnp.float32,
    )
    numer = (
        numer
        + own_weight.astype(jnp.bfloat16).astype(jnp.float32)[..., None]
        * fresh_value.astype(jnp.float32)[:, :, None, :]
    )
    return (numer / total[..., None], top + jnp.log(total))


def prompt_partial(query_vector, key_rows, value_rows, live_length):
    scale = 1.0 / math.sqrt(query_vector.shape[-1])
    scores = (
        jnp.einsum("skgd,tkd->kgst", query_vector, key_rows, preferred_element_type=jnp.float32)
        * scale
    )
    live = jnp.arange(key_rows.shape[0], dtype=jnp.int32)[None, None, None, :] < live_length
    scores = jnp.where(live, scores, -jnp.inf)
    top = jnp.max(scores, axis=-1)
    weights = jnp.where(live, jnp.exp(scores - top[..., None]), 0.0)
    total = jnp.sum(weights, axis=-1)
    numer = jnp.einsum(
        "kgst,tkd->skgd",
        weights.astype(jnp.bfloat16),
        value_rows,
        preferred_element_type=jnp.float32,
    )
    total_s = jnp.transpose(total, (2, 0, 1))
    attention_output = (numer / total_s[..., None]).astype(jnp.bfloat16)
    log_sum_exp = jnp.transpose(top, (2, 0, 1)) + jnp.log(total_s)
    return (attention_output, log_sum_exp)


def shards(
    hidden_in,
    norm_gain,
    w_query,
    key_projection,
    value_projection,
    w_out,
    pre_keys,
    prompt_values,
    continuation_keys,
    continuation_values,
    group_seq,
    request_order,
    pre_len,
    continuation_length,
):
    request_rows = hidden_in.shape[0]
    n_req = lax.axis_size("req")
    total_rows = request_rows * n_req
    head_dim = HEAD_SIZE
    local_kv = key_projection.shape[1] // head_dim
    prompt_weight = QUERY_HEADS // KEY_VALUE_HEADS
    local_heads = local_kv * prompt_weight
    query_cols = local_heads * head_dim
    local_groups = pre_keys.shape[0]
    prompt_len = pre_keys.shape[1]
    tail_cap = continuation_keys.shape[1]
    all_groups = pre_len.shape[0]
    req_index = lax.axis_index("req")
    group_of = jnp.zeros((total_rows,), jnp.int32).at[request_order].set(group_seq)
    own_groups = lax.dynamic_slice_in_dim(group_of, req_index * request_rows, request_rows)
    table_hit = own_groups[:, None] == jnp.arange(all_groups, dtype=jnp.int32)[None, :]
    own_prompt = jnp.sum(jnp.where(table_hit, pre_len[None, :], 0), axis=1)
    token_position = own_prompt + continuation_length
    hidden32 = hidden_in.astype(jnp.float32)
    normalized_hidden = (
        hidden32
        * lax.rsqrt(jnp.mean(hidden32 * hidden32, axis=1, keepdims=True) + EPS)
        * norm_gain.astype(jnp.float32)
    ).astype(jnp.bfloat16)
    query_vector = apply_rotary(
        jnp.dot(normalized_hidden, w_query, preferred_element_type=jnp.float32).reshape(
            request_rows, local_heads, head_dim
        ),
        token_position,
    ).astype(jnp.bfloat16)
    fresh_key = apply_rotary(
        jnp.dot(normalized_hidden, key_projection, preferred_element_type=jnp.float32).reshape(
            request_rows, local_kv, head_dim
        ),
        token_position,
    ).astype(jnp.bfloat16)
    fresh_value = (
        jnp.dot(normalized_hidden, value_projection, preferred_element_type=jnp.float32)
        .reshape(request_rows, local_kv, head_dim)
        .astype(jnp.bfloat16)
    )
    query_flattened = query_vector.reshape(request_rows, query_cols)
    query_all = lax.all_gather(query_flattened, "req", axis=0, tiled=True)
    first_group = req_index * local_groups
    group_ids = first_group + jnp.arange(local_groups, dtype=jnp.int32)
    member = group_of[None, :] == group_ids[:, None]
    rank = jnp.cumsum(member.astype(jnp.int32), axis=1) - 1
    slot_ids = jnp.arange(GROUP_CAPACITY, dtype=jnp.int32)
    select_group = member[:, None, :] & (rank[:, None, :] == slot_ids[None, :, None])
    selected_rows = jnp.einsum(
        "jsr,rq->jsq",
        select_group.astype(jnp.bfloat16),
        query_all,
        preferred_element_type=jnp.float32,
    ).astype(jnp.bfloat16)
    selected_rows = selected_rows.reshape(
        local_groups, GROUP_CAPACITY, local_kv, prompt_weight, head_dim
    )
    lengths = lax.dynamic_slice_in_dim(pre_len, first_group, local_groups)
    keys4 = pre_keys.reshape(local_groups, prompt_len, local_kv, head_dim)
    values4 = prompt_values.reshape(local_groups, prompt_len, local_kv, head_dim)
    continuation_output, continuation_log_sum = continuation_partial(
        query_vector.reshape(request_rows, local_kv, prompt_weight, head_dim),
        fresh_key,
        fresh_value,
        continuation_keys.reshape(request_rows, tail_cap, local_kv, head_dim),
        continuation_values.reshape(request_rows, tail_cap, local_kv, head_dim),
        continuation_length,
    )
    group_out, group_lse = jax.vmap(prompt_partial)(selected_rows, keys4, values4, lengths)
    pick32 = select_group.astype(jnp.float32)
    full_lse = jnp.einsum(
        "jsr,jsh->rh",
        pick32,
        group_lse.reshape(local_groups, GROUP_CAPACITY, local_heads),
        precision=lax.Precision.HIGHEST,
    )
    full_out = jnp.einsum(
        "jsr,jsq->rq",
        pick32,
        group_out.reshape(local_groups, GROUP_CAPACITY, query_cols).astype(jnp.float32),
        precision=lax.Precision.HIGHEST,
    )
    sectioned_out = full_out.reshape(n_req, request_rows, query_cols)
    sectioned_lse = full_lse.reshape(n_req, request_rows, local_heads)
    got_out, got_lse = (
        lax.all_to_all(sectioned_out, "req", split_axis=0, concat_axis=0, tiled=True),
        lax.all_to_all(sectioned_lse, "req", split_axis=0, concat_axis=0, tiled=True),
    )
    pre_out = jnp.sum(got_out, axis=0)
    pre_lse = jnp.sum(got_lse, axis=0)
    tail_lse2 = continuation_log_sum.reshape(request_rows, local_heads)
    both = jnp.logaddexp(pre_lse, tail_lse2)
    attn = jnp.exp(pre_lse - both)[..., None] * pre_out.reshape(
        request_rows, local_heads, head_dim
    ) + jnp.exp(tail_lse2 - both)[..., None] * continuation_output.reshape(
        request_rows, local_heads, head_dim
    )
    attn = attn.reshape(request_rows, query_cols).astype(jnp.bfloat16)
    partial_out = jnp.dot(attn, w_out, preferred_element_type=jnp.float32)
    return lax.psum_scatter(partial_out, "kv", scatter_dimension=1, tiled=True).astype(jnp.bfloat16)


def solution(mesh):
    placed = (
        P("req", None),
        P(),
        P(None, "kv"),
        P(None, "kv"),
        P(None, "kv"),
        P("kv", None),
        P("req", None, "kv"),
        P("req", None, "kv"),
        P("req", None, "kv"),
        P("req", None, "kv"),
        P(),
        P(),
        P(),
        P("req"),
    )
    return jax.shard_map(
        shards, mesh=mesh, in_specs=placed, out_specs=P("req", "kv"), check_vma=False
    )
```

profile of v0, /device:TPU:0, one launch (start us, length us, event | category | flops | bytes accessed | tf_op | source)
XLA Modules:
  0.0 166.1 jit_solution(11495850110260666148)
XLA Ops:
  8.1 1.3 fusion.21
  9.5 7.4 %fusion.92 = f32[64,1280]{1,0:T(8,128)S(1)} fusion(bf16[5120,1280]{1,0:T(8,128)(2,1)} %param.16, bf16[64,5120]{1,0:T(8,128)(2,1)} %param.14, f32[5120]{0:T(1024)S(1)} %convert_element_type.71, f32[64]{0:T(128)S(1)} %add_rsqrt_fusion), kind=kOutput, calls=%fused_computation.114 | convolution fusion | flops 840171520 | bytes 14110976 | tf_op jit(solution)/shard_map/dot_general | solution.py:130
  16.9 2.8 %scatter_custom_fusion = s32[512]{0:T(512)S(1)} fusion(s32[512]{0:T(512)S(1)} %compare_select_fusion, s32[512]{0:T(512)} %param.24, s32[]{:T(128)} %constant.14.clone.1), kind=kCustom, calls=%fused_computation.100 | custom fusion | bytes 2560 | tf_op jit(solution)/shard_map/scatter | solution.py:118
  22.1 1.6 copy.89
  24.4 1.8 %reduce-window.6 = s32[6,4,128]{2,1,0:T(4,128)S(1)} reduce-window(s32[6,4,128]{2,1,0:T(4,128)S(1)} %compare_convert_fusion, s32[]{:T(128)} %constant.14.clone.1), window={size=1x1x128 pad=0_0x0_0x127_0}, to_apply=%region_1.2 | reduce-window | flops 390144 | bytes 24580 | tf_op jit(solution)/shard_map/reduce-window
  27.3 9.8 %reshape.304 = bf16[6,2048,2,128]{3,2,1,0:T(2,128)(2,1)} reshape(bf16[6,2048,256]{2,1,0:T(8,128)(2,1)} %param.20) | data formatting | bytes 12582912 | tf_op jit(solution)/shard_map/reshape | solution.py:164
  37.1 9.9 %reshape.309 = bf16[6,2048,2,128]{3,2,1,0:T(2,128)(2,1)} reshape(bf16[6,2048,256]{2,1,0:T(8,128)(2,1)} %param.21) | data formatting | bytes 12582912 | tf_op jit(solution)/shard_map/reshape | solution.py:165
  54.4 1.6 convolution_convert_fusion
  56.3 5.8 %bitcast_reduce_fusion = (f32[6,2,5,16]{3,2,1,0:T(8,128)S(1)}, f32[6,2,16,5,2048]{4,2,3,1,0:T(8,128)S(1)}) fusion(pred[6,2048]{1,0:T(8,128)(4,1)S(1)} %iota_compare_fusion.2, bf16[6,2048,2,128,1]{3,2,1,0,4:T(2,128)(2,1)} %bitcast.129, bf16[6,16,2,5,128]{4,3,2,1,0:T(8,128)(2,1)S(1)} %reshape.303), kind=kOutput, calls=%fused_computation.2 | convolution fusion | flops 509213760 | bytes 14417664 | tf_op jit(solution)/shard_map/vmap(skgd,tkd->kgst)/dot_general | solution.py:69
  62.1 2.3 %fusion.7 = f32[6,2,5,16]{3,2,1,0:T(8,128)S(1)} fusion(f32[6,2,16,5,2048]{4,2,3,1,0:T(8,128)S(1)} %get-tuple-element.22, f32[6,2,5,16]{3,2,1,0:T(8,128)S(1)} %get-tuple-element.21, pred[6,2048]{1,0:T(8,128)(4,1)S(1)} %iota_compare_fusion.2), kind=kLoop, calls=%fused_computation.11 | loop fusion | flops 9829440 | bytes 7884288 | tf_op jit(solution)/shard_map/vmap()/reduce_sum | solution.py:76
  64.4 5.5 %fusion.48 = bf16[6,16,2,5,128]{4,1,3,2,0:T(8,128)(2,1)S(1)} fusion(bf16[6,2048,2,128,1]{3,2,1,0,4:T(2,128)(2,1)} %bitcast.130, f32[6,2,16,5,2048]{4,2,3,1,0:T(8,128)S(1)} %get-tuple-element.22, f32[6,2,5,16]{3,2,1,0:T(8,128)S(1)} %get-tuple-element.21, pred[6,2048]{1,0:T(8,128)(4,1)S(1)} %iota_compare_fusion.2, f32[6,16,2,5]{1,3,2,0:T(8,128)S(1)} %bitcast.137), kind=kOutput, calls=%fused_computation.41 | convolution fusion | flops 513392640 | bytes 14421504 | tf_op jit(solution)/shard_map/vmap(kgst,tkd->skgd)/dot_general | solution.py:77
  71.3 5.1 %all-to-all-start = ((f32[8,1,640]{2,1,0:T(1,128)}), f32[8,1,640]{2,1,0:T(1,128)S(1)}, u32[]{:S(2)}, u32[]{:S(2)}) async-start(f32[8,1,640]{2,1,0:T(1,128)} %reshape.335), calls=%async_computation | async-start | bytes 40960 | tf_op jit(solution)/shard_map/all_to_all | solution.py:192
  76.5 2.1 %convolution_bitcast_fusion = f32[8,64,1280]{2,1,0:T(8,128)} fusion(bf16[6,16,1280,1]{2,1,0,3:T(8,128)(2,1)S(1)} %reshape.330, pred[8,64,6,16]{1,0,3,2:T(8,128)(4,1)S(1)} %copy-done.6), kind=kOutput, calls=%fused_computation.18 | convolution fusion | flops 125829120 | bytes 2916352 | tf_op jit(solution)/shard_map/jsr,jsq->rq/dot_general | solution.py:182
  78.5 2.7 %all-to-all-done = f32[8,1,640]{2,1,0:T(1,128)S(1)} async-done(((f32[8,1,640]{2,1,0:T(1,128)}), f32[8,1,640]{2,1,0:T(1,128)S(1)}, u32[]{:S(2)}, u32[]{:S(2)}) %all-to-all-start) | async-done | bytes 20512 | tf_op jit(solution)/shard_map/all_to_all | solution.py:192
  81.8 3.6 %all-to-all-start.1 = ((f32[8,64,1280]{2,1,0:T(8,128)}), f32[8,64,1280]{2,1,0:T(8,128)S(1)}, u32[]{:S(2)}, u32[]{:S(2)}) async-start(f32[8,64,1280]{2,1,0:T(8,128)} %convolution_bitcast_fusion), calls=%async_computation.1 | async-start | bytes 5242880 | tf_op jit(solution)/shard_map/all_to_all | solution.py:191
  86.5 4.4 %fusion.96 = (f32[64,2,5]{2,1,0:T(2,128)}, f32[64,2,5,64]{3,2,1,0:T(8,128)}) fusion(bf16[64,2,5,64]{3,2,1,0:T(8,128)(2,1)} %copy-done.4, bf16[64,2,5,64]{3,2,1,0:T(8,128)(2,1)S(1)} %copy.91, pred[64,64]{1,0:T(8,128)(4,1)S(1)} %iota_compare_fusion.3, bf16[64,64,256]{2,1,0:T(8,128)(2,1)} %param.22), kind=kOutput, calls=%fused_computation.115 | convolution fusion | flops 10935680 | bytes 2431488 | tf_op jit(solution)/shard_map/rkgd,rtkd->rkgt/dot_general | solution.py:36
  92.6 1.4 fusion.54
  95.1 2.4 %fusion.42 = f32[64,256]{1,0:T(8,128)S(1)} fusion(bf16[5120,256]{1,0:T(8,128)(2,1)} %param.18, bf16[64,5120]{1,0:T(8,128)(2,1)S(1)} %copy-done.2, f32[5120]{0:T(1024)} %copy-done.5, f32[64]{0:T(128)} %copy-done.13), kind=kOutput, calls=%fused_computation.39 | convolution fusion | flops 169115648 | bytes 3363072 | tf_op jit(solution)/shard_map/dot_general | solution.py:142
  97.5 3.3 %fusion.34 = f32[64,2,5,128]{3,2,1,0:T(8,128)} fusion(f32[64,2,5,64]{3,2,1,0:T(8,128)} %get-tuple-element.20, f32[64,2,5]{2,1,0:T(2,128)S(1)} %copy.105, f32[64,2,128]{2,1,0:T(2,128)S(1)} %reshape.313, f32[64,2,5]{2,1,0:T(2,128)S(1)} %copy.104, f32[64,2,5]{2,1,0:T(2,128)S(1)} %copy.95, pred[64,64]{1,0:T(8,128)(4,1)S(1)} %iota_compare_fusion.3, ...), kind=kOutput, calls=%fused_computation.35 | convolution fusion | flops 10854400 | bytes 2665984 | tf_op jit(solution)/shard_map/rkgt,rtkd->rkgd/dot_general | solution.py:52
  100.8 1.1 reshape.312
  103.5 14.2 %all-to-all-done.1 = f32[8,64,1280]{2,1,0:T(8,128)S(1)} async-done(((f32[8,64,1280]{2,1,0:T(8,128)}), f32[8,64,1280]{2,1,0:T(8,128)S(1)}, u32[]{:S(2)}, u32[]{:S(2)}) %all-to-all-start.1) | async-done | bytes 2621472 | tf_op jit(solution)/shard_map/all_to_all | solution.py:191
  118.2 8.5 %fusion.67 = f32[64,5120]{1,0:T(8,128)} fusion(bf16[1280,5120]{1,0:T(8,128)(2,1)} %param.19, f32[64,1280]{1,0:T(8,128)S(1)} %reshape.312, f32[8,8,10,128]{3,2,1,0:T(8,128)S(1)} %bitcast.132, f32[64,1280]{1,0:T(8,128)S(1)} %reduce_sum.59, f32[8,8,10,128]{3,2,1,0:T(8,128)S(1)} %bitcast.131), kind=kOutput, calls=%fused_computation.63 | convolution fusion | flops 839188480 | bytes 15728640 | tf_op jit(solution)/shard_map/dot_general | solution.py:204
  126.7 30.8 %reduce-scatter.2.cloned.1.call-done = f32[64,1280]{1,0:T(8,128)} async-done(((f32[64,5120]{1,0:T(8,128)}), f32[64,1280]{1,0:T(8,128)}) %reduce-scatter.2.cloned.1.call-update) | async-done | bytes 327696 | tf_op jit(solution)/shard_map/reduce_scatter | solution.py:205
  157.6 1.7 convert_element_type.85
  (103 shorter events, 21.0 us)
Async XLA Ops:
  6.5 41.4 %copy-start = (bf16[5120,256]{1,0:T(8,128)(2,1)S(1)}, bf16[5120,256]{1,0:T(8,128)(2,1)}, u32[]{:S(2)}) copy-start(bf16[5120,256]{1,0:T(8,128)(2,1)} %param.17) | copy-start | bytes 7864324
  6.5 47.8 %all-gather.2.cloned.1.call-start = ((), (), s32[]{:S(2)}) async-start(), calls=%async_computation.3 | async-start | bytes 1474560 | tf_op jit(solution)/shard_map/all_gather | solution.py:147
  8.1 39.8 %copy-start.5 = (f32[5120]{0:T(1024)}, f32[5120]{0:T(1024)S(1)}, u32[]{:S(2)}) copy-start(f32[5120]{0:T(1024)S(1)} %convert_element_type.71) | copy-start | bytes 61444
  9.4 38.5 %copy-start.13 = (f32[64]{0:T(128)}, f32[64]{0:T(128)S(1)}, u32[]{:S(2)}) copy-start(f32[64]{0:T(128)S(1)} %add_rsqrt_fusion) | copy-start | bytes 772
  9.4 10.4 %copy-start.16 = (s32[48]{0:T(128)S(1)}, s32[48]{0:T(128)}, u32[]{:S(2)}) copy-start(s32[48]{0:T(128)} %param.26) | copy-start | bytes 580
  9.5 10.5 %copy-start.15 = (s32[64]{0:T(128)S(1)}, s32[64]{0:T(128)}, u32[]{:S(2)}) copy-start(s32[64]{0:T(128)} %param.27) | copy-start | bytes 772
  19.7 27.3 %copy-start.12 = (s32[512]{0:T(512)}, s32[512]{0:T(512)S(1)}, u32[]{:S(2)}) copy-start(s32[512]{0:T(512)S(1)} %scatter_custom_fusion) | copy-start | bytes 6148
  20.1 17.0 %copy-start.7 = (f32[64,64]{1,0:T(8,128)}, f32[64,64]{1,0:T(8,128)S(1)}, u32[]{:S(2)}) copy-start(f32[64,64]{1,0:T(8,128)S(1)} %get-tuple-element.17) | copy-start | bytes 49156
  20.1 17.0 %copy-start.8 = (f32[64,64]{1,0:T(8,128)}, f32[64,64]{1,0:T(8,128)S(1)}, u32[]{:S(2)}) copy-start(f32[64,64]{1,0:T(8,128)S(1)} %get-tuple-element.18) | copy-start | bytes 49156
  20.4 0.7 copy-start.3
  22.0 25.0 %copy-start.14 = (s32[6]{0:T(128)}, s32[6]{0:T(128)S(1)}, u32[]{:S(2)}) copy-start(s32[6]{0:T(128)S(1)} %iota_add_fusion) | copy-start | bytes 76
  37.1 10.8 %copy-start.2 = (bf16[64,5120]{1,0:T(8,128)(2,1)S(1)}, bf16[64,5120]{1,0:T(8,128)(2,1)}, u32[]{:S(2)}) copy-start(bf16[64,5120]{1,0:T(8,128)(2,1)} %param.14) | copy-start | bytes 1966084
  50.7 3.7 %copy-start.4 = (bf16[64,2,5,64]{3,2,1,0:T(8,128)(2,1)}, bf16[64,2,5,64]{3,2,1,0:T(8,128)(2,1)S(1)}, u32[]{:S(2)}) copy-start(bf16[64,2,5,64]{3,2,1,0:T(8,128)(2,1)S(1)} %copy.92) | copy-start | bytes 245764
  64.4 6.0 %copy-start.6 = (pred[8,64,6,16]{1,0,3,2:T(8,128)(4,1)S(1)}, pred[8,64,6,16]{1,0,3,2:T(8,128)(4,1)}, u32[]{:S(2)}) copy-start(pred[8,64,6,16]{1,0,3,2:T(8,128)(4,1)} %and.27) | copy-start | bytes 147460
  71.3 9.9 %all-to-all-start = ((f32[8,1,640]{2,1,0:T(1,128)}), f32[8,1,640]{2,1,0:T(1,128)S(1)}, u32[]{:S(2)}, u32[]{:S(2)}) async-start(f32[8,1,640]{2,1,0:T(1,128)} %reshape.335), calls=%async_computation | async-start | bytes 40960 | tf_op jit(solution)/shard_map/all_to_all | solution.py:192
  81.2 0.6 copy-start.9
  81.8 35.8 %all-to-all-start.1 = ((f32[8,64,1280]{2,1,0:T(8,128)}), f32[8,64,1280]{2,1,0:T(8,128)S(1)}, u32[]{:S(2)}, u32[]{:S(2)}) async-start(f32[8,64,1280]{2,1,0:T(8,128)} %convolution_bitcast_fusion), calls=%async_computation.1 | async-start | bytes 5242880 | tf_op jit(solution)/shard_map/all_to_all | solution.py:191
  85.5 6.4 %copy-start.11 = (f32[64,2,1,5]{0,1,3,2:T(2,128)S(1)}, f32[64,2,1,5]{0,1,3,2:T(2,128)}, u32[]{:S(2)}) copy-start(f32[64,2,1,5]{0,1,3,2:T(2,128)} %copy.109) | copy-start | bytes 7684
  85.5 72.1 %reduce-scatter.2.cloned.1.call-start = ((), (), s32[]{:S(2)}) async-start(), calls=%async_computation.4 | async-start | bytes 1638400 | tf_op jit(solution)/shard_map/reduce_scatter | solution.py:205
  97.5 4.9 %copy-start.10 = (f32[8,1,640]{2,1,0:T(1,128)S(1)}, f32[8,1,640]{2,1,0:T(1,128)}, u32[]{:S(2)}) copy-start(f32[8,1,640]{2,1,0:T(1,128)} %copy-done.9) | copy-start | bytes 61444
  118.2 41.0 %copy-start.1 = (bf16[5120,256]{1,0:T(8,128)(2,1)S(1)}, bf16[5120,256]{1,0:T(8,128)(2,1)}, u32[]{:S(2)}) copy-start(bf16[5120,256]{1,0:T(8,128)(2,1)} %param.17) | copy-start | bytes 7864324
Sparse Core Ops, SparseCore 0:
  22.1 27.2 all-gather.1
  126.9 30.6 reduce-scatter.1
where the time goes:
time: 167 us; the launch traced here: 166 us
  waiting for transfers between devices  47.8 us (29%)
  matrix products  42.2 us (25%)
  local copies, waits for them, and re-layouts  37.3 us (22%)
  other arithmetic  15.9 us (10%)
  between operations  13.9 us (8%)
  starting transfers between devices  9.02 us (5%)
    reduce_scatter x1, waiting for transfers between devices, shards(): lax.psum_scatter(partial_out, 'kv', scatter_dimension=1, tiled=True)  30.8 us
    all_to_all x1, waiting for transfers between devices, shards(): lax.all_to_all(sectioned_out, 'req', split_axis=0, concat_axis=0, tiled=T...  14.2 us
    reshape x1, local copies, waits for them, and re-layouts, shards(): prompt_values.reshape(local_groups, prompt_len, local_kv, head_dim)  9.88 us
    reshape x1, local copies, waits for them, and re-layouts, shards(): keys4 = pre_keys.reshape(local_groups, prompt_len, local_kv, head_dim)  9.78 us
    dot_general x1, matrix products, shards(): partial_out = jnp.dot(attn, w_out, preferred_element_type=jnp.float32)  8.49 us
    dot_general x1, matrix products, shards(): jnp.dot(normalized_hidden, w_query, preferred_element_type=jnp.float32)  7.4 us
    dot_general x1, matrix products, prompt_partial(): jnp.einsum('skgd,tkd->kgst', query_vector, key_rows, preferred_element_ty...  5.76 us
    dot_general x1, matrix products, prompt_partial(): jnp.einsum('kgst,tkd->skgd', weights.astype(jnp.bfloat16), value_rows, pr...  5.55 us
  transfers between devices with their start and end apart: 4, of which 3 were waited for; matrix products, arithmetic and copies ran while one was open for 31% of the time, Pallas kernels for 0%

commit v1 on v0

v1 whole, which is shorter than its diff:
```python
import functools
import math

import jax
import jax.numpy as jnp
from jax import lax
from jax.experimental import pallas as pl
from jax.experimental.pallas import tpu as pltpu
from jax.sharding import PartitionSpec as P

HEAD_SIZE = 128
QUERY_PER_KEY = 5
GROUP_CAPACITY = 16
EPS = 1e-06
THETA = 1000000.0
NEG = -1e30
FAST_CAPACITY = 32
CHUNK_ROWS = 16

F32 = jnp.float32
BF16 = jnp.bfloat16
MESH = pl.DeviceIdType.MESH


def iota(shape, dim):
    return lax.broadcasted_iota(jnp.int32, shape, dim)


def to_row(col):
    n = col.shape[0]
    eye = iota((n, n), 0) == iota((n, n), 1)
    return jnp.sum(jnp.where(eye, col, 0.0), axis=0, keepdims=True)


def to_col(row):
    n = row.shape[1]
    eye = iota((n, n), 0) == iota((n, n), 1)
    return jnp.sum(jnp.where(eye, row, 0.0), axis=1, keepdims=True)


def onehot(mask):
    return jnp.where(mask, 1.0, 0.0).astype(BF16)


def body(
    cap,
    n,
    nkv,
    gain_ref,
    order_ref,
    group_ref,
    plen_ref,
    clen_ref,
    hidden_hbm,
    wq_hbm,
    wk_hbm,
    wv_hbm,
    wo_hbm,
    pk_hbm,
    pv_hbm,
    ck_hbm,
    cv_hbm,
    out_ref,
    hidden,
    normed,
    w,
    wo,
    pk,
    pv,
    ck,
    cv,
    qkv,
    sel,
    packed,
    sendq,
    recvq,
    sendo,
    recvo,
    tail_out,
    tail_lse,
    attn,
    zsend,
    zrecv,
    h_sem,
    w_sem,
    wo_sem,
    pk_sem,
    pv_sem,
    ck_sem,
    cv_sem,
    q_send_sem,
    q_recv_sem,
    o_send_sem,
    o_recv_sem,
    z_send_sem,
    z_recv_sem,
):
    rows = hidden.shape[0]
    lg = pk.shape[0]
    plen = pk.shape[1]
    chunk = w.shape[2]
    lkv = chunk // HEAD_SIZE
    heads = lkv * QUERY_PER_KEY
    qc = heads * HEAD_SIZE
    tcap = ck.shape[0] // rows
    oc = out_ref.shape[1]
    slots = lg * GROUP_CAPACITY
    total = order_ref.shape[1]
    scale = 1.0 / math.sqrt(HEAD_SIZE)
    me = lax.axis_index("req")
    mk = lax.axis_index("kv")

    h_copy = pltpu.make_async_copy(hidden_hbm, hidden, h_sem)
    h_copy.start()
    for i in range(QUERY_PER_KEY):
        pltpu.make_async_copy(wq_hbm.at[:, pl.ds(i * chunk, chunk)], w.at[i], w_sem.at[i]).start()
    pltpu.make_async_copy(wk_hbm, w.at[QUERY_PER_KEY], w_sem.at[QUERY_PER_KEY]).start()
    pltpu.make_async_copy(wv_hbm, w.at[QUERY_PER_KEY + 1], w_sem.at[QUERY_PER_KEY + 1]).start()

    barrier = pltpu.get_barrier_semaphore()
    for o in range(1, n):
        pl.semaphore_signal(
            barrier, inc=1, device_id=(lax.rem(me + o, n), mk), device_id_type=MESH
        )
    for o in range(1, nkv):
        pl.semaphore_signal(
            barrier, inc=1, device_id=(me, lax.rem(mk + o, nkv)), device_id_type=MESH
        )

    order = order_ref[...].astype(F32)
    groups = group_ref[...].astype(F32)
    plens = plen_ref[...].astype(F32)
    lane = iota((1, total), 1).astype(F32)

    own = iota((rows, 1), 0).astype(F32) + (me * rows).astype(F32)
    g_col = jnp.sum(jnp.where(order == own, groups, 0.0), axis=1, keepdims=True)
    all_g = iota((1, plens.shape[1]), 1).astype(F32)
    own_len = jnp.sum(jnp.where(all_g == g_col, plens, 0.0), axis=1, keepdims=True)
    position = own_len + clen_ref[...].astype(F32)
    d_col = jnp.floor((g_col + 0.5) * (1.0 / lg))
    d_row = to_row(d_col)
    earlier = (d_col == d_row) & (iota((rows, rows), 0) < iota((rows, rows), 1))
    t_row = d_row * cap + jnp.sum(jnp.where(earlier, 1.0, 0.0), axis=0, keepdims=True)
    t_col = to_col(t_row)
    to_send = onehot(iota((n * cap, rows), 0).astype(F32) == t_row)
    from_return = onehot(iota((rows, n * cap), 1).astype(F32) == t_col)

    slot = iota((slots, 1), 0).astype(F32)
    slot_g = jnp.floor((slot + 0.5) * (1.0 / GROUP_CAPACITY))
    slot_k = slot - slot_g * GROUP_CAPACITY
    slot_g = slot_g + (me * lg).astype(F32)
    start = jnp.sum(jnp.where(groups < slot_g, 1.0, 0.0), axis=1, keepdims=True)
    count = jnp.sum(jnp.where(groups == slot_g, 1.0, 0.0), axis=1, keepdims=True)
    r_col = jnp.sum(jnp.where(lane == start + slot_k, order, 0.0), axis=1, keepdims=True)
    live = slot_k < count
    s_col = jnp.where(live, jnp.floor((r_col + 0.5) * (1.0 / rows)), -1.0)
    same = (s_col == to_row(s_col)) & (to_row(r_col) < r_col)
    u_col = jnp.where(
        live, s_col * cap + jnp.sum(jnp.where(same, 1.0, 0.0), axis=1, keepdims=True), -1.0
    )
    from_query = onehot(iota((slots, n * cap), 1).astype(F32) == u_col)
    to_return = onehot(iota((n * cap, slots), 0).astype(F32) == to_row(u_col))

    half = HEAD_SIZE // 2
    lane_h = iota((1, HEAD_SIZE), 1)
    upper = lane_h >= half
    freq_index = jnp.where(upper, lane_h - half, lane_h).astype(F32)
    freq = jnp.exp(-math.log(THETA) * 2.0 * freq_index / HEAD_SIZE)
    angle = position * freq
    cosine = jnp.cos(angle)
    sine = jnp.where(upper, jnp.sin(angle), -jnp.sin(angle))

    h_copy.wait()
    h32 = hidden[...].astype(F32)
    inv = lax.rsqrt(jnp.mean(h32 * h32, axis=1, keepdims=True) + EPS)
    normed[...] = (h32 * inv * gain_ref[...].astype(F32)).astype(BF16)

    def project(i, carry):
        pltpu.make_async_copy(wk_hbm, w.at[i], w_sem.at[i]).wait()
        y = jnp.dot(normed[...], w[i], preferred_element_type=F32)
        for a in range(lkv):
            x = y[:, a * HEAD_SIZE : (a + 1) * HEAD_SIZE]
            turned = x * cosine + pltpu.roll(x, half, 1) * sine
            x = jnp.where(i == QUERY_PER_KEY + 1, x, turned)
            qkv[i, :, a * HEAD_SIZE : (a + 1) * HEAD_SIZE] = x.astype(BF16)
        return carry

    lax.fori_loop(0, 3, project, 0)
    pltpu.make_async_copy(ck_hbm, ck, ck_sem).start()
    pltpu.make_async_copy(cv_hbm, cv, cv_sem).start()
    for g in range(lg):
        pltpu.make_async_copy(pk_hbm.at[g], pk.at[g], pk_sem.at[g]).start()
        pltpu.make_async_copy(pv_hbm.at[g], pv.at[g], pv_sem.at[g]).start()
    for j in range(nkv):
        pltpu.make_async_copy(wo_hbm.at[:, pl.ds(j * oc, oc)], wo.at[j], wo_sem.at[j]).start()
    lax.fori_loop(3, QUERY_PER_KEY, project, 0)

    for i in range(QUERY_PER_KEY):
        sendq[:, i * chunk : (i + 1) * chunk] = jnp.dot(
            to_send, qkv[i], preferred_element_type=F32
        ).astype(BF16)
    pl.semaphore_wait(barrier, n - 1 + nkv - 1)

    def req_copy(src, dst, send_sem, recv_sem, o):
        to = lax.rem(me + o, n)
        return pltpu.make_async_remote_copy(
            src_ref=src.at[pl.ds(pl.multiple_of(to * cap, cap), cap)],
            dst_ref=dst.at[pl.ds(pl.multiple_of(me * cap, cap), cap)],
            send_sem=send_sem.at[o],
            recv_sem=recv_sem.at[me],
            device_id=(to, mk),
            device_id_type=MESH,
        )

    def req_arrival(src, dst, send_sem, recv_sem, o):
        frm = lax.rem(me + n - o, n)
        here = pl.ds(pl.multiple_of(frm * cap, cap), cap)
        return pltpu.make_async_remote_copy(
            src_ref=src.at[here],
            dst_ref=dst.at[here],
            send_sem=send_sem.at[o],
            recv_sem=recv_sem.at[frm],
            device_id=(frm, mk),
            device_id_type=MESH,
        )

    mine = pl.ds(pl.multiple_of(me * cap, cap), cap)
    for o in range(1, n):
        req_copy(sendq, recvq, q_send_sem, q_recv_sem, o).start()
    recvq[mine, :] = sendq[mine, :]

    lax.fori_loop(QUERY_PER_KEY, QUERY_PER_KEY + 2, project, 0)
    pltpu.make_async_copy(ck_hbm, ck, ck_sem).wait()
    pltpu.make_async_copy(cv_hbm, cv, cv_sem).wait()
    block = CHUNK_ROWS
    width = block * tcap
    q_rows = QUERY_PER_KEY * block
    lanes = iota((block, HEAD_SIZE), 1)
    row_r = lax.rem(iota((q_rows, 1), 0), block)
    low = row_r * tcap
    col_t = iota((1, width), 1)

    def own_part(b, carry):
        at = pl.ds(pl.multiple_of(b * block, block), block)
        kv_at = pl.ds(pl.multiple_of(b * width, width), width)
        length = clen_ref[at, :]
        length = jnp.concatenate([length] * QUERY_PER_KEY, axis=0)
        ok = (col_t >= low) & (col_t < low + length)
        lse_tile = jnp.zeros((block, HEAD_SIZE), F32)
        for k in range(lkv):
            ks = slice(k * HEAD_SIZE, (k + 1) * HEAD_SIZE)
            parts = []
            for h in range(QUERY_PER_KEY):
                head = k * QUERY_PER_KEY + h
                c, a = head // lkv, head % lkv
                parts.append(qkv[c, at, a * HEAD_SIZE : (a + 1) * HEAD_SIZE])
            q = jnp.concatenate(parts, axis=0)
            new_k = qkv[QUERY_PER_KEY, at, ks].astype(F32)
            new_v = qkv[QUERY_PER_KEY + 1, at, ks].astype(F32)
            s = lax.dot_general(
                q, ck[kv_at, ks], (((1,), (1,)), ((), ())), preferred_element_type=F32
            ) * scale
            s = jnp.where(ok, s, NEG)
            fresh = jnp.sum(
                q.astype(F32) * jnp.concatenate([new_k] * QUERY_PER_KEY, axis=0),
                axis=1,
                keepdims=True,
            ) * scale
            top = jnp.maximum(jnp.max(s, axis=1, keepdims=True), fresh)
            e = jnp.exp(s - top)
            fresh_e = jnp.exp(fresh - top)
            l = jnp.sum(e, axis=1, keepdims=True) + fresh_e
            acc = jnp.dot(e.astype(BF16), cv[kv_at, ks], preferred_element_type=F32)
            acc = acc + fresh_e.astype(BF16).astype(F32) * jnp.concatenate(
                [new_v] * QUERY_PER_KEY, axis=0
            )
            acc = acc / l
            lse = top + jnp.log(l)
            for h in range(QUERY_PER_KEY):
                head = k * QUERY_PER_KEY + h
                rs = slice(h * block, (h + 1) * block)
                tail_out[at, head * HEAD_SIZE : (head + 1) * HEAD_SIZE] = acc[rs]
                lse_tile = jnp.where(lanes == head, lse[rs], lse_tile)
        tail_lse[at, :] = lse_tile
        return carry

    lax.fori_loop(0, rows // block, own_part, 0)

    for o in range(1, n):
        req_arrival(sendq, recvq, q_send_sem, q_recv_sem, o).wait_recv()
    sel[...] = jnp.dot(from_query, recvq[...], preferred_element_type=F32).astype(BF16)

    cap_g = GROUP_CAPACITY
    lanes_g = iota((cap_g, HEAD_SIZE), 1)
    part_of = lanes_g // 32
    lane_of = lanes_g - part_of * 32
    col_p = iota((1, plen), 1).astype(F32)

    def prompt_part(g, carry):
        pltpu.make_async_copy(pk_hbm.at[g], pk.at[g], pk_sem.at[g]).wait()
        pltpu.make_async_copy(pv_hbm.at[g], pv.at[g], pv_sem.at[g]).wait()
        at = pl.ds(pl.multiple_of(g * cap_g, cap_g), cap_g)
        gid = (me * lg + g).astype(F32)
        length = jnp.sum(jnp.where(all_g == gid, plens, 0.0), axis=1, keepdims=True)
        ok = col_p < length
        lse_tile = jnp.zeros((cap_g, HEAD_SIZE), F32)
        for k in range(lkv):
            ks = slice(k * HEAD_SIZE, (k + 1) * HEAD_SIZE)
            q = jnp.concatenate(
                [
                    sel[at, (k * QUERY_PER_KEY + h) * HEAD_SIZE : (k * QUERY_PER_KEY + h + 1) * HEAD_SIZE]
                    for h in range(QUERY_PER_KEY)
                ],
                axis=0,
            )
            s = lax.dot_general(
                q, pk[g, :, ks], (((1,), (1,)), ((), ())), preferred_element_type=F32
            ) * scale
            s = jnp.where(ok, s, NEG)
            top = jnp.max(s, axis=1, keepdims=True)
            e = jnp.exp(s - top)
            l = jnp.sum(e, axis=1, keepdims=True)
            acc = jnp.dot(e.astype(BF16), pv[g, :, ks], preferred_element_type=F32) / l
            lse = top + jnp.log(l)
            for h in range(QUERY_PER_KEY):
                head = k * QUERY_PER_KEY + h
                rs = slice(h * cap_g, (h + 1) * cap_g)
                packed[at, head * HEAD_SIZE : (head + 1) * HEAD_SIZE] = acc[rs].astype(BF16)
                lse_tile = jnp.where(lane_of == head, lse[rs], lse_tile)
        hi = lse_tile.astype(BF16).astype(F32)
        mid = (lse_tile - hi).astype(BF16).astype(F32)
        low_part = lse_tile - hi - mid
        tile = jnp.where(part_of == 0, hi, jnp.where(part_of == 1, mid, low_part))
        packed[at, qc : qc + HEAD_SIZE] = jnp.where(part_of == 3, 0.0, tile).astype(BF16)
        return carry

    lax.fori_loop(0, lg, prompt_part, 0)

    sendo[...] = jnp.dot(to_return, packed[...], preferred_element_type=F32).astype(BF16)
    for o in range(1, n):
        req_copy(sendo, recvo, o_send_sem, o_recv_sem, o).start()
    recvo[mine, :] = sendo[mine, :]
    for j in range(nkv):
        pltpu.make_async_copy(
            wo_hbm.at[:, pl.ds(j * oc, oc)], wo.at[j], wo_sem.at[j]
        ).wait()
    for o in range(1, n):
        req_arrival(sendo, recvo, o_send_sem, o_recv_sem, o).wait_recv()
    got = jnp.dot(from_return, recvo[...], preferred_element_type=F32)

    parts = got[:, qc : qc + HEAD_SIZE]
    pre_lse = parts + pltpu.roll(parts, HEAD_SIZE - 32, 1) + pltpu.roll(parts, HEAD_SIZE - 64, 1)
    t_lse = tail_lse[...]
    top = jnp.maximum(pre_lse, t_lse)
    both = top + jnp.log(jnp.exp(pre_lse - top) + jnp.exp(t_lse - top))
    w_pre = jnp.exp(pre_lse - both)
    w_tail = jnp.exp(t_lse - both)
    for head in range(heads):
        hs = slice(head * HEAD_SIZE, (head + 1) * HEAD_SIZE)
        attn[:, hs] = (
            w_pre[:, head : head + 1] * got[:, hs] + w_tail[:, head : head + 1] * tail_out[:, hs]
        ).astype(BF16)

    def z_copy(o):
        return pltpu.make_async_remote_copy(
            src_ref=zsend.at[o - 1],
            dst_ref=zrecv.at[o - 1],
            send_sem=z_send_sem.at[o - 1],
            recv_sem=z_recv_sem.at[o - 1],
            device_id=(me, lax.rem(mk + o, nkv)),
            device_id_type=MESH,
        )

    for o in range(1, nkv):
        zsend[o - 1] = jnp.dot(
            attn[...], wo[lax.rem(mk + o, nkv)], preferred_element_type=F32
        ).astype(BF16)
        z_copy(o).start()
    acc = jnp.dot(attn[...], wo[mk], preferred_element_type=F32)
    for o in range(1, nkv):
        z_copy(o).wait_recv()
        acc = acc + zrecv[o - 1].astype(F32)
    out_ref[...] = acc.astype(BF16)
    for o in range(1, n):
        req_copy(sendq, recvq, q_send_sem, q_recv_sem, o).wait_send()
        req_copy(sendo, recvo, o_send_sem, o_recv_sem, o).wait_send()
    for o in range(1, nkv):
        z_copy(o).wait_send()


def attend(cap, n, nkv, cid, *arrays):
    (gain, order, group, plen, clen, hidden, wq, wk, wv, wo, pk, pv, ck, cv) = arrays
    rows, model = hidden.shape
    chunk = wk.shape[1]
    qc = wq.shape[1]
    oc = wo.shape[1] // nkv
    lg, positions = pk.shape[0], pk.shape[1]
    slots = lg * GROUP_CAPACITY
    wide = qc + HEAD_SIZE
    vmem = pl.BlockSpec(memory_space=pltpu.VMEM)
    hbm = pl.BlockSpec(memory_space=pl.ANY)
    dma = pltpu.SemaphoreType.DMA
    return pl.pallas_call(
        functools.partial(body, cap, n, nkv),
        out_shape=jax.ShapeDtypeStruct((rows, oc), BF16),
        in_specs=[vmem] * 5 + [hbm] * 9,
        out_specs=vmem,
        scratch_shapes=[
            pltpu.VMEM((rows, model), BF16),
            pltpu.VMEM((rows, model), BF16),
            pltpu.VMEM((QUERY_PER_KEY + 2, model, chunk), BF16),
            pltpu.VMEM((nkv, qc, oc), BF16),
            pltpu.VMEM(pk.shape, BF16),
            pltpu.VMEM(pv.shape, BF16),
            pltpu.VMEM(ck.shape, BF16),
            pltpu.VMEM(cv.shape, BF16),
            pltpu.VMEM((QUERY_PER_KEY + 2, rows, chunk), BF16),
            pltpu.VMEM((slots, qc), BF16),
            pltpu.VMEM((slots, wide), BF16),
            pltpu.VMEM((n * cap, qc), BF16),
            pltpu.VMEM((n * cap, qc), BF16),
            pltpu.VMEM((n * cap, wide), BF16),
            pltpu.VMEM((n * cap, wide), BF16),
            pltpu.VMEM((rows, qc), F32),
            pltpu.VMEM((rows, HEAD_SIZE), F32),
            pltpu.VMEM((rows, qc), BF16),
            pltpu.VMEM((nkv - 1, rows, oc), BF16),
            pltpu.VMEM((nkv - 1, rows, oc), BF16),
            dma,
            dma((QUERY_PER_KEY + 2,)),
            dma((nkv,)),
            dma((lg,)),
            dma((lg,)),
            dma,
            dma,
            dma((n,)),
            dma((n,)),
            dma((n,)),
            dma((n,)),
            dma((nkv - 1,)),
            dma((nkv - 1,)),
        ],
        compiler_params=pltpu.CompilerParams(
            collective_id=cid, has_side_effects=True, vmem_limit_bytes=62 * 1024 * 1024
        ),
        name="attend%d" % cap,
    )(*arrays)


def shards(
    hidden_in,
    norm_gain,
    w_query,
    key_projection,
    value_projection,
    w_out,
    pre_keys,
    prompt_values,
    continuation_keys,
    continuation_values,
    group_seq,
    request_order,
    pre_len,
    continuation_length,
):
    n = lax.axis_size("req")
    nkv = lax.axis_size("kv")
    rows = hidden_in.shape[0]
    lg = pre_keys.shape[0]
    width = continuation_keys.shape[2]
    arrays = (
        norm_gain[None, :],
        request_order[None, :],
        group_seq[None, :],
        pre_len[None, :],
        continuation_length[:, None],
        hidden_in,
        w_query,
        key_projection,
        value_projection,
        w_out,
        pre_keys,
        prompt_values,
        continuation_keys.reshape(-1, width),
        continuation_values.reshape(-1, width),
    )
    if rows <= FAST_CAPACITY:
        return attend(rows, n, nkv, 0, *arrays)
    pair = (request_order // rows) * n + group_seq // lg
    counts = jnp.sum(
        (pair[None, :] == jnp.arange(n * n, dtype=jnp.int32)[:, None]).astype(jnp.int32), axis=1
    )
    return lax.cond(
        jnp.max(counts) <= FAST_CAPACITY,
        functools.partial(attend, FAST_CAPACITY, n, nkv, 0),
        functools.partial(attend, rows, n, nkv, 1),
        *arrays,
    )


def solution(mesh):
    placed = (
        P("req", None),
        P(),
        P(None, "kv"),
        P(None, "kv"),
        P(None, "kv"),
        P("kv", None),
        P("req", None, "kv"),
        P("req", None, "kv"),
        P("req", None, "kv"),
        P("req", None, "kv"),
        P(),
        P(),
        P(),
        P("req"),
    )
    return jax.shard_map(
        shards, mesh=mesh, in_specs=placed, out_specs=P("req", "kv"), check_vma=False
    )
```

time: 167 us -> 62.9 us (0.38)
  the two profiles are of different devices: /device:TPU:0 before, /device:TPU:9 now
where the time goes in v1:
time: 62.9 us; the launch traced here: 62.6 us
  Pallas kernels  57 us (91%)
  local copies, waits for them, and re-layouts  3.34 us (5%)
  other arithmetic  1.46 us (2%)
  between operations  0.67 us (1%)
    pallas_call x1, Pallas kernels, attend(): pl.pallas_call(functools.partial(body, cap, n, nkv), out_shape=jax.ShapeD...  57 us
    broadcast_in_dim x1, local copies, waits for them, and re-layouts, shards(): continuation_length[:, None]  1.36 us
    broadcast_in_dim x1, local copies, waits for them, and re-layouts, shards(): norm_gain[None, :]  1.31 us

profile of v1, /device:TPU:9, one launch (start us, length us, event | category | flops | bytes accessed | tf_op | source)
XLA Modules:
  0.0 62.6 jit_solution(17071775403501087511)
XLA Ops:
  0.0 0.7 %fusion = s32[512]{0:T(512)S(1)} fusion(s32[512]{0:T(512)} %param.26, s32[512]{0:T(512)} %param.27), kind=kLoop, calls=%fused_computation.7 | loop fusion | flops 12800 | bytes 6144 | tf_op jit(solution)/shard_map/add | solution.py:489
  0.7 0.1 convert_reduce_fusion
  0.8 0.6 %reduce_max.9 = s32[]{:T(128)} reduce(s32[64]{0:T(128)S(1)} %convert_reduce_fusion, s32[]{:T(128)} %constant.26.clone.1), dimensions={0}, to_apply=%region_1.2 | reduce | flops 63 | bytes 264 | tf_op jit(solution)/shard_map/reduce_max | solution.py:494
  2.1 59.8 %conditional.1 = (bf16[64,1280]{1,0:T(8,128)(2,1)S(1)}) conditional(s32[]{:T(128)} %convert_element_type.7, (bf16[5120]{0:T(1024)(128)(2,1)}, s32[512]{0:T(512)}, s32[512]{0:T(512)}, s32[48]{0:T(128)}, s32[64]{0:T(128)}, /*index=5*/bf16[64,5120]{1,0:T(8,128)(2,1)}, bf16[5120,1280]{1,0:T(8,128)(2,1)}, bf16[5120,256]{1,0:T(8,128)(2,1)}, ...), branch_computations={%region_2.3_spmd, %region_3.4_spmd} | conditional | bytes 21000 | solution.py:493
  2.3 1.3 %broadcast_in_dim.23.gain_ref = bf16[1,5120]{1,0:T(2,128)(2,1)} reshape(bf16[5120]{0:T(1024)(128)(2,1)} %get-tuple-element.146) | data formatting | bytes 20480 | tf_op jit(solution)/shard_map/broadcast_in_dim | solution.py:472
  3.6 1.4 %copy.44.clen_ref = s32[64,1]{1,0:T(8,128)} copy(s32[64,1]{0,1:T(1,128)} %bitcast.23) | data formatting | bytes 512 | tf_op jit(solution)/shard_map/broadcast_in_dim | solution.py:476
  5.0 57.0 %attend32.1 = bf16[64,1280]{1,0:T(8,128)(2,1)S(1)} custom-call(bf16[1,5120]{1,0:T(2,128)(2,1)} %broadcast_in_dim.23.gain_ref, s32[1,512]{1,0:T(1,128)} %bitcast.19, s32[1,512]{1,0:T(1,128)} %bitcast.17, s32[1,48]{1,0:T(1,128)} %bitcast.21, s32[64,1]{1,0:T(8,128)} %copy.44.clen_ref, bf16[64,5120]{1,0:T(8,128)(2,1)} %get-tuple-element.128.hidden_hbm, ...), custom_call_target="tpu_custom_call" | custom-call | tf_op jit(solution)/shard_map/cond/branch_1_fun/attend32/pallas_call | solution.py:403
  62.0 0.7 %copy.48 = bf16[64,1280]{1,0:T(8,128)(2,1)} copy(bf16[64,1280]{1,0:T(8,128)(2,1)S(1)} %get-tuple-element.92) | data formatting | bytes 327680

commit v2 on v1

--- a/solution.py
+++ b/solution.py
@@ -63,13 +63,17 @@
     out_ref,
     hidden,
     normed,
-    w,
+    wq,
+    wkv,
     wo,
     pk,
     pv,
     ck,
     cv,
-    qkv,
+    acc_q,
+    query,
+    new_kv,
+    lengths,
     sel,
     packed,
     sendq,
@@ -98,7 +102,7 @@
     rows = hidden.shape[0]
     lg = pk.shape[0]
     plen = pk.shape[1]
-    chunk = w.shape[2]
+    chunk = wkv.shape[2]
     lkv = chunk // HEAD_SIZE
     heads = lkv * QUERY_PER_KEY
     qc = heads * HEAD_SIZE
@@ -112,10 +116,18 @@
 
     h_copy = pltpu.make_async_copy(hidden_hbm, hidden, h_sem)
     h_copy.start()
+    k_rows = hidden.shape[1] // QUERY_PER_KEY
+
+    def wq_copy(i):
+        at = pl.ds(pl.multiple_of(i * k_rows, k_rows), k_rows)
+        return pltpu.make_async_copy(wq_hbm.at[at], wq.at[at], w_sem.at[i])
+
+    wk_copy = pltpu.make_async_copy(wk_hbm, wkv.at[0], w_sem.at[QUERY_PER_KEY])
+    wv_copy = pltpu.make_async_copy(wv_hbm, wkv.at[1], w_sem.at[QUERY_PER_KEY + 1])
     for i in range(QUERY_PER_KEY):
-        pltpu.make_async_copy(wq_hbm.at[:, pl.ds(i * chunk, chunk)], w.at[i], w_sem.at[i]).start()
-    pltpu.make_async_copy(wk_hbm, w.at[QUERY_PER_KEY], w_sem.at[QUERY_PER_KEY]).start()
-    pltpu.make_async_copy(wv_hbm, w.at[QUERY_PER_KEY + 1], w_sem.at[QUERY_PER_KEY + 1]).start()
+        wq_copy(i).start()
+    wk_copy.start()
+    wv_copy.start()
 
     barrier = pltpu.get_barrier_semaphore()
     for o in range(1, n):
@@ -136,7 +148,9 @@
     g_col = jnp.sum(jnp.where(order == own, groups, 0.0), axis=1, keepdims=True)
     all_g = iota((1, plens.shape[1]), 1).astype(F32)
     own_len = jnp.sum(jnp.where(all_g == g_col, plens, 0.0), axis=1, keepdims=True)
-    position = own_len + clen_ref[...].astype(F32)
+    own_tail = to_col(clen_ref[...].astype(F32))
+    lengths[...] = jnp.broadcast_to(own_tail, lengths.shape)
+    position = own_len + own_tail
     d_col = jnp.floor((g_col + 0.5) * (1.0 / lg))
     d_row = to_row(d_col)
     earlier = (d_col == d_row) & (iota((rows, rows), 0) < iota((rows, rows), 1))
@@ -173,63 +187,88 @@
     h_copy.wait()
     h32 = hidden[...].astype(F32)
     inv = lax.rsqrt(jnp.mean(h32 * h32, axis=1, keepdims=True) + EPS)
-    normed[...] = (h32 * inv * gain_ref[...].astype(F32)).astype(BF16)
+    normed[...] = (h32 * inv * gain_ref[...].astype(F32)[None, :]).astype(BF16)
+
+    def turned(y, head):
+        x = y[:, head * HEAD_SIZE : (head + 1) * HEAD_SIZE]
+        return (x * cosine + pltpu.roll(x, half, 1) * sine).astype(BF16)
 
     def project(i, carry):
-        pltpu.make_async_copy(wk_hbm, w.at[i], w_sem.at[i]).wait()
-        y = jnp.dot(normed[...], w[i], preferred_element_type=F32)
-        for a in range(lkv):
-            x = y[:, a * HEAD_SIZE : (a + 1) * HEAD_SIZE]
-            turned = x * cosine + pltpu.roll(x, half, 1) * sine
-            x = jnp.where(i == QUERY_PER_KEY + 1, x, turned)
-            qkv[i, :, a * HEAD_SIZE : (a + 1) * HEAD_SIZE] = x.astype(BF16)
+        wq_copy(i).wait()
+        at = pl.ds(pl.multiple_of(i * k_rows, k_rows), k_rows)
+        acc_q[...] += jnp.dot(normed[:, at], wq[at, :], preferred_element_type=F32)
         return carry
 
+    acc_q[...] = jnp.zeros(acc_q.shape, F32)
     lax.fori_loop(0, 3, project, 0)
-    pltpu.make_async_copy(ck_hbm, ck, ck_sem).start()
-    pltpu.make_async_copy(cv_hbm, cv, cv_sem).start()
     for g in range(lg):
         pltpu.make_async_copy(pk_hbm.at[g], pk.at[g], pk_sem.at[g]).start()
         pltpu.make_async_copy(pv_hbm.at[g], pv.at[g], pv_sem.at[g]).start()
-    for j in range(nkv):
-        pltpu.make_async_copy(wo_hbm.at[:, pl.ds(j * oc, oc)], wo.at[j], wo_sem.at[j]).start()
+        if g == 0:
+            pltpu.make_async_copy(ck_hbm, ck, ck_sem).start()
+            pltpu.make_async_copy(cv_hbm, cv, cv_sem).start()
     lax.fori_loop(3, QUERY_PER_KEY, project, 0)
-
-    for i in range(QUERY_PER_KEY):
-        sendq[:, i * chunk : (i + 1) * chunk] = jnp.dot(
-            to_send, qkv[i], preferred_element_type=F32
-        ).astype(BF16)
+    for head in range(heads):
+        query[:, head * HEAD_SIZE : (head + 1) * HEAD_SIZE] = turned(acc_q, head)
+
+    sendq[...] = jnp.dot(to_send, query[...], preferred_element_type=F32).astype(BF16)
     pl.semaphore_wait(barrier, n - 1 + nkv - 1)
 
-    def req_copy(src, dst, send_sem, recv_sem, o):
+    def q_copy(o):
         to = lax.rem(me + o, n)
         return pltpu.make_async_remote_copy(
-            src_ref=src.at[pl.ds(pl.multiple_of(to * cap, cap), cap)],
-            dst_ref=dst.at[pl.ds(pl.multiple_of(me * cap, cap), cap)],
-            send_sem=send_sem.at[o],
-            recv_sem=recv_sem.at[me],
+            src_ref=sendq.at[pl.ds(pl.multiple_of(to * cap, cap), cap)],
+            dst_ref=recvq.at[pl.ds(pl.multiple_of(me * cap, cap), cap)],
+            send_sem=q_send_sem.at[o],
+            recv_sem=q_recv_sem.at[o],
             device_id=(to, mk),
             device_id_type=MESH,
         )
 
-    def req_arrival(src, dst, send_sem, recv_sem, o):
-        frm = lax.rem(me + n - o, n)
-        here = pl.ds(pl.multiple_of(frm * cap, cap), cap)
+    def q_arrival(o):
+        here = pl.ds(pl.multiple_of(lax.rem(me + n - o, n) * cap, cap), cap)
         return pltpu.make_async_remote_copy(
-            src_ref=src.at[here],
-            dst_ref=dst.at[here],
-            send_sem=send_sem.at[o],
-            recv_sem=recv_sem.at[frm],
-            device_id=(frm, mk),
+            src_ref=sendq.at[here],
+            dst_ref=recvq.at[here],
+            send_sem=q_send_sem.at[o],
+            recv_sem=q_recv_sem.at[o],
+            device_id=(lax.rem(me + o, n), mk),
+            device_id_type=MESH,
+        )
+
+    def o_copy(k, o):
+        to = lax.rem(me + o, n)
+        return pltpu.make_async_remote_copy(
+            src_ref=sendo.at[k, pl.ds(pl.multiple_of(to * cap, cap), cap)],
+            dst_ref=recvo.at[k, pl.ds(pl.multiple_of(me * cap, cap), cap)],
+            send_sem=o_send_sem.at[k, o],
+            recv_sem=o_recv_sem.at[k, o],
+            device_id=(to, mk),
+            device_id_type=MESH,
+        )
+
+    def o_arrival(k, o):
+        here = pl.ds(pl.multiple_of(lax.rem(me + n - o, n) * cap, cap), cap)
+        return pltpu.make_async_remote_copy(
+            src_ref=sendo.at[k, here],
+            dst_ref=recvo.at[k, here],
+            send_sem=o_send_sem.at[k, o],
+            recv_sem=o_recv_sem.at[k, o],
+            device_id=(lax.rem(me + o, n), mk),
             device_id_type=MESH,
         )
 
     mine = pl.ds(pl.multiple_of(me * cap, cap), cap)
     for o in range(1, n):
-        req_copy(sendq, recvq, q_send_sem, q_recv_sem, o).start()
+        q_copy(o).start()
     recvq[mine, :] = sendq[mine, :]
 
-    lax.fori_loop(QUERY_PER_KEY, QUERY_PER_KEY + 2, project, 0)
+    wk_copy.wait()
+    y = jnp.dot(normed[...], wkv[0], preferred_element_type=F32)
+    for k in range(lkv):
+        new_kv[0, :, k * HEAD_SIZE : (k + 1) * HEAD_SIZE] = turned(y, k)
+    wv_copy.wait()
+    new_kv[1] = jnp.dot(normed[...], wkv[1], preferred_element_type=F32).astype(BF16)
     pltpu.make_async_copy(ck_hbm, ck, ck_sem).wait()
     pltpu.make_async_copy(cv_hbm, cv, cv_sem).wait()
     block = CHUNK_ROWS
@@ -243,20 +282,19 @@
     def own_part(b, carry):
         at = pl.ds(pl.multiple_of(b * block, block), block)
         kv_at = pl.ds(pl.multiple_of(b * width, width), width)
-        length = clen_ref[at, :]
+        length = lengths[at, 0:1].astype(jnp.int32)
         length = jnp.concatenate([length] * QUERY_PER_KEY, axis=0)
         ok = (col_t >= low) & (col_t < low + length)
-        lse_tile = jnp.zeros((block, HEAD_SIZE), F32)
         for k in range(lkv):
+            lse_tile = jnp.zeros((block, HEAD_SIZE), F32)
             ks = slice(k * HEAD_SIZE, (k + 1) * HEAD_SIZE)
             parts = []
             for h in range(QUERY_PER_KEY):
                 head = k * QUERY_PER_KEY + h
-                c, a = head // lkv, head % lkv
-                parts.append(qkv[c, at, a * HEAD_SIZE : (a + 1) * HEAD_SIZE])
+                parts.append(query[at, head * HEAD_SIZE : (head + 1) * HEAD_SIZE])
             q = jnp.concatenate(parts, axis=0)
-            new_k = qkv[QUERY_PER_KEY, at, ks].astype(F32)
-            new_v = qkv[QUERY_PER_KEY + 1, at, ks].astype(F32)
+            new_k = new_kv[0, at, ks].astype(F32)
+            new_v = new_kv[1, at, ks].astype(F32)
             s = lax.dot_general(
                 q, ck[kv_at, ks], (((1,), (1,)), ((), ())), preferred_element_type=F32
             ) * scale
@@ -280,14 +318,16 @@
                 head = k * QUERY_PER_KEY + h
                 rs = slice(h * block, (h + 1) * block)
                 tail_out[at, head * HEAD_SIZE : (head + 1) * HEAD_SIZE] = acc[rs]
-                lse_tile = jnp.where(lanes == head, lse[rs], lse_tile)
-        tail_lse[at, :] = lse_tile
+                lse_tile = jnp.where(lanes == h, lse[rs], lse_tile)
+            tail_lse[k, at, :] = lse_tile
         return carry
 
     lax.fori_loop(0, rows // block, own_part, 0)
 
     for o in range(1, n):
-        req_arrival(sendq, recvq, q_send_sem, q_recv_sem, o).wait_recv()
+        q_arrival(o).wait_recv()
+    for j in range(nkv):
+        pltpu.make_async_copy(wo_hbm.at[:, pl.ds(j * oc, oc)], wo.at[j], wo_sem.at[j]).start()
     sel[...] = jnp.dot(from_query, recvq[...], preferred_element_type=F32).astype(BF16)
 
     cap_g = GROUP_CAPACITY
@@ -296,70 +336,83 @@
     lane_of = lanes_g - part_of * 32
     col_p = iota((1, plen), 1).astype(F32)
 
-    def prompt_part(g, carry):
-        pltpu.make_async_copy(pk_hbm.at[g], pk.at[g], pk_sem.at[g]).wait()
-        pltpu.make_async_copy(pv_hbm.at[g], pv.at[g], pv_sem.at[g]).wait()
+    pc = QUERY_PER_KEY * HEAD_SIZE
+    log2e = 1.0 / math.log(2.0)
+    step = 2 if lg % 2 == 0 else 1
+
+    def prompt_part(k, g):
         at = pl.ds(pl.multiple_of(g * cap_g, cap_g), cap_g)
         gid = (me * lg + g).astype(F32)
         length = jnp.sum(jnp.where(all_g == gid, plens, 0.0), axis=1, keepdims=True)
         ok = col_p < length
+        ks = slice(k * HEAD_SIZE, (k + 1) * HEAD_SIZE)
+        q = jnp.concatenate(
+            [
+                sel[at, k * pc + h * HEAD_SIZE : k * pc + (h + 1) * HEAD_SIZE]
+                for h in range(QUERY_PER_KEY)
+            ],
+            axis=0,
+        )
+        s = lax.dot_general(
+            q, pk[g, :, ks], (((1,), (1,)), ((), ())), preferred_element_type=F32
+        ) * (scale * log2e)
+        s = jnp.where(ok, s, NEG)
+        top = jnp.max(s, axis=1, keepdims=True)
+        e = jnp.exp2(s - top)
+        l = jnp.sum(e, axis=1, keepdims=True)
+        acc = jnp.dot(e.astype(BF16), pv[g, :, ks], preferred_element_type=F32) / l
+        lse = top * math.log(2.0) + jnp.log(l)
         lse_tile = jnp.zeros((cap_g, HEAD_SIZE), F32)
-        for k in range(lkv):
-            ks = slice(k * HEAD_SIZE, (k + 1) * HEAD_SIZE)
-            q = jnp.concatenate(
-                [
-                    sel[at, (k * QUERY_PER_KEY + h) * HEAD_SIZE : (k * QUERY_PER_KEY + h + 1) * HEAD_SIZE]
-                    for h in range(QUERY_PER_KEY)
-                ],
-                axis=0,
-            )
-            s = lax.dot_general(
-                q, pk[g, :, ks], (((1,), (1,)), ((), ())), preferred_element_type=F32
-            ) * scale
-            s = jnp.where(ok, s, NEG)
-            top = jnp.max(s, axis=1, keepdims=True)
-            e = jnp.exp(s - top)
-            l = jnp.sum(e, axis=1, keepdims=True)
-            acc = jnp.dot(e.astype(BF16), pv[g, :, ks], preferred_element_type=F32) / l
-            lse = top + jnp.log(l)
-            for h in range(QUERY_PER_KEY):
-                head = k * QUERY_PER_KEY + h
-                rs = slice(h * cap_g, (h + 1) * cap_g)
-                packed[at, head * HEAD_SIZE : (head + 1) * HEAD_SIZE] = acc[rs].astype(BF16)
-                lse_tile = jnp.where(lane_of == head, lse[rs], lse_tile)
+        for h in range(QUERY_PER_KEY):
+            rs = slice(h * cap_g, (h + 1) * cap_g)
+            packed[at, h * HEAD_SIZE : (h + 1) * HEAD_SIZE] = acc[rs].astype(BF16)
+            lse_tile = jnp.where(lane_of == h, lse[rs], lse_tile)
         hi = lse_tile.astype(BF16).astype(F32)
         mid = (lse_tile - hi).astype(BF16).astype(F32)
         low_part = lse_tile - hi - mid
         tile = jnp.where(part_of == 0, hi, jnp.where(part_of == 1, mid, low_part))
-        packed[at, qc : qc + HEAD_SIZE] = jnp.where(part_of == 3, 0.0, tile).astype(BF16)
-        return carry
-
-    lax.fori_loop(0, lg, prompt_part, 0)
-
-    sendo[...] = jnp.dot(to_return, packed[...], preferred_element_type=F32).astype(BF16)
-    for o in range(1, n):
-        req_copy(sendo, recvo, o_send_sem, o_recv_sem, o).start()
-    recvo[mine, :] = sendo[mine, :]
+        packed[at, pc : pc + HEAD_SIZE] = jnp.where(part_of == 3, 0.0, tile).astype(BF16)
+
+    for k in range(lkv):
+
+        def prompt_step(j, carry, k=k):
+            if k == 0:
+                for a in range(step):
+                    g = j * step + a
+                    pltpu.make_async_copy(pk_hbm.at[g], pk.at[g], pk_sem.at[g]).wait()
+                    pltpu.make_async_copy(pv_hbm.at[g], pv.at[g], pv_sem.at[g]).wait()
+            for a in range(step):
+                prompt_part(k, j * step + a)
+            return carry
+
+        lax.fori_loop(0, lg // step, prompt_step, 0)
+        sendo[k] = jnp.dot(to_return, packed[...], preferred_element_type=F32).astype(BF16)
+        for o in range(1, n):
+            o_copy(k, o).start()
+        recvo[k, mine, :] = sendo[k, mine, :]
+
     for j in range(nkv):
         pltpu.make_async_copy(
             wo_hbm.at[:, pl.ds(j * oc, oc)], wo.at[j], wo_sem.at[j]
         ).wait()
-    for o in range(1, n):
-        req_arrival(sendo, recvo, o_send_sem, o_recv_sem, o).wait_recv()
-    got = jnp.dot(from_return, recvo[...], preferred_element_type=F32)
-
-    parts = got[:, qc : qc + HEAD_SIZE]
-    pre_lse = parts + pltpu.roll(parts, HEAD_SIZE - 32, 1) + pltpu.roll(parts, HEAD_SIZE - 64, 1)
-    t_lse = tail_lse[...]
-    top = jnp.maximum(pre_lse, t_lse)
-    both = top + jnp.log(jnp.exp(pre_lse - top) + jnp.exp(t_lse - top))
-    w_pre = jnp.exp(pre_lse - both)
-    w_tail = jnp.exp(t_lse - both)
-    for head in range(heads):
-        hs = slice(head * HEAD_SIZE, (head + 1) * HEAD_SIZE)
-        attn[:, hs] = (
-            w_pre[:, head : head + 1] * got[:, hs] + w_tail[:, head : head + 1] * tail_out[:, hs]
-        ).astype(BF16)
+
+    for k in range(lkv):
+        for o in range(1, n):
+            o_arrival(k, o).wait_recv()
+        got = jnp.dot(from_return, recvo[k], preferred_element_type=F32)
+        parts = got[:, pc : pc + HEAD_SIZE]
+        pre_lse = parts + pltpu.roll(parts, HEAD_SIZE - 32, 1) + pltpu.roll(parts, HEAD_SIZE - 64, 1)
+        t_lse = tail_lse[k]
+        top = jnp.maximum(pre_lse, t_lse)
+        both = top + jnp.log(jnp.exp(pre_lse - top) + jnp.exp(t_lse - top))
+        w_pre = jnp.exp(pre_lse - both)
+        w_tail = jnp.exp(t_lse - both)
+        for h in range(QUERY_PER_KEY):
+            hs = slice(k * pc + h * HEAD_SIZE, k * pc + (h + 1) * HEAD_SIZE)
+            attn[:, hs] = (
+                w_pre[:, h : h + 1] * got[:, h * HEAD_SIZE : (h + 1) * HEAD_SIZE]
+                + w_tail[:, h : h + 1] * tail_out[:, hs]
+            ).astype(BF16)
 
     def z_copy(o):
         return pltpu.make_async_remote_copy(
@@ -382,8 +435,9 @@
         acc = acc + zrecv[o - 1].astype(F32)
     out_ref[...] = acc.astype(BF16)
     for o in range(1, n):
-        req_copy(sendq, recvq, q_send_sem, q_recv_sem, o).wait_send()
-        req_copy(sendo, recvo, o_send_sem, o_recv_sem, o).wait_send()
+        q_copy(o).wait_send()
+        for k in range(lkv):
+            o_copy(k, o).wait_send()
     for o in range(1, nkv):
         z_copy(o).wait_send()
 
@@ -396,7 +450,8 @@
     oc = wo.shape[1] // nkv
     lg, positions = pk.shape[0], pk.shape[1]
     slots = lg * GROUP_CAPACITY
-    wide = qc + HEAD_SIZE
+    lkv = chunk // HEAD_SIZE
+    wide = QUERY_PER_KEY * HEAD_SIZE + HEAD_SIZE
     vmem = pl.BlockSpec(memory_space=pltpu.VMEM)
     hbm = pl.BlockSpec(memory_space=pl.ANY)
     dma = pltpu.SemaphoreType.DMA
@@ -408,21 +463,25 @@
         scratch_shapes=[
             pltpu.VMEM((rows, model), BF16),
             pltpu.VMEM((rows, model), BF16),
-            pltpu.VMEM((QUERY_PER_KEY + 2, model, chunk), BF16),
+            pltpu.VMEM((model, qc), BF16),
+            pltpu.VMEM((2, model, chunk), BF16),
             pltpu.VMEM((nkv, qc, oc), BF16),
             pltpu.VMEM(pk.shape, BF16),
             pltpu.VMEM(pv.shape, BF16),
             pltpu.VMEM(ck.shape, BF16),
             pltpu.VMEM(cv.shape, BF16),
-            pltpu.VMEM((QUERY_PER_KEY + 2, rows, chunk), BF16),
+            pltpu.VMEM((rows, qc), F32),
+            pltpu.VMEM((rows, qc), BF16),
+            pltpu.VMEM((2, rows, chunk), BF16),
+            pltpu.VMEM((rows, HEAD_SIZE), F32),
             pltpu.VMEM((slots, qc), BF16),
             pltpu.VMEM((slots, wide), BF16),
             pltpu.VMEM((n * cap, qc), BF16),
             pltpu.VMEM((n * cap, qc), BF16),
-            pltpu.VMEM((n * cap, wide), BF16),
-            pltpu.VMEM((n * cap, wide), BF16),
+            pltpu.VMEM((lkv, n * cap, wide), BF16),
+            pltpu.VMEM((lkv, n * cap, wide), BF16),
             pltpu.VMEM((rows, qc), F32),
-            pltpu.VMEM((rows, HEAD_SIZE), F32),
+            pltpu.VMEM((lkv, rows, HEAD_SIZE), F32),
             pltpu.VMEM((rows, qc), BF16),
             pltpu.VMEM((nkv - 1, rows, oc), BF16),
             pltpu.VMEM((nkv - 1, rows, oc), BF16),
@@ -435,8 +494,8 @@
             dma,
             dma((n,)),
             dma((n,)),
-            dma((n,)),
-            dma((n,)),
+            dma((lkv, n)),
+            dma((lkv, n)),
             dma((nkv - 1,)),
             dma((nkv - 1,)),
         ],
@@ -469,11 +528,11 @@
     lg = pre_keys.shape[0]
     width = continuation_keys.shape[2]
     arrays = (
-        norm_gain[None, :],
+        norm_gain,
         request_order[None, :],
         group_seq[None, :],
         pre_len[None, :],
-        continuation_length[:, None],
+        continuation_length[None, :],
         hidden_in,
         w_query,
         key_projection,

time: 62.9 us -> 55.9 us (0.89)
  Pallas kernels: 57 us -> 52.7 us
  local copies, waits for them, and re-layouts: 3.34 us -> 0.67 us
    pallas_call x1, Pallas kernels: 57 us -> 52.7 us  [attend(): pl.pallas_call(functools.partial(body, cap, n, nkv), out_shape=jax.ShapeD...]
    broadcast_in_dim x2 -> x0, local copies, waits for them, and re-layouts: 2.67 us -> none  [the longest x1 1.36 us: shards(): continuation_length[:, None]]
where the time goes in v2:
time: 55.9 us; the launch traced here: 55.7 us
  Pallas kernels  52.7 us (94%)
  other arithmetic  1.46 us (3%)
  local copies, waits for them, and re-layouts  0.67 us (1%)
  between operations  0.67 us (1%)
    pallas_call x1, Pallas kernels, attend(): pl.pallas_call(functools.partial(body, cap, n, nkv), out_shape=jax.ShapeD...  52.7 us

profile of v2, /device:TPU:9, one launch (start us, length us, event | category | flops | bytes accessed | tf_op | source)
XLA Modules:
  0.0 55.7 jit_solution(2979743309463299834)
XLA Ops:
  0.0 0.7 %fusion = s32[512]{0:T(512)S(1)} fusion(s32[512]{0:T(512)} %param.26, s32[512]{0:T(512)} %param.27), kind=kLoop, calls=%fused_computation.7 | loop fusion | flops 12800 | bytes 6144 | tf_op jit(solution)/shard_map/add | solution.py:548
  0.7 0.1 convert_reduce_fusion
  0.8 0.6 %reduce_max.9 = s32[]{:T(128)} reduce(s32[64]{0:T(128)S(1)} %convert_reduce_fusion, s32[]{:T(128)} %constant.26.clone.1), dimensions={0}, to_apply=%region_1.2 | reduce | flops 63 | bytes 264 | tf_op jit(solution)/shard_map/reduce_max | solution.py:553
  2.1 52.9 %conditional.1 = (bf16[64,1280]{1,0:T(8,128)(2,1)S(1)}) conditional(s32[]{:T(128)} %convert_element_type.7, (bf16[5120]{0:T(1024)(128)(2,1)}, s32[512]{0:T(512)}, s32[512]{0:T(512)}, s32[48]{0:T(128)}, s32[64]{0:T(128)}, /*index=5*/bf16[64,5120]{1,0:T(8,128)(2,1)}, bf16[5120,1280]{1,0:T(8,128)(2,1)}, bf16[5120,256]{1,0:T(8,128)(2,1)}, ...), branch_computations={%region_2.3_spmd, %region_3.4_spmd} | conditional | bytes 8 | solution.py:552
  2.3 52.7 %attend32.1 = bf16[64,1280]{1,0:T(8,128)(2,1)S(1)} custom-call(bf16[5120]{0:T(1024)(128)(2,1)} %get-tuple-element.122.gain_ref, s32[1,512]{1,0:T(1,128)} %bitcast.19, s32[1,512]{1,0:T(1,128)} %bitcast.17, s32[1,48]{1,0:T(1,128)} %bitcast.21, s32[1,64]{1,0:T(1,128)} %bitcast.23, bf16[64,5120]{1,0:T(8,128)(2,1)} %get-tuple-element.128.hidden_hbm, ...), custom_call_target="tpu_custom_call" | custom-call | tf_op jit(solution)/shard_map/cond/branch_1_fun/attend32/pallas_call | solution.py:458
  55.1 0.7 %copy.44 = bf16[64,1280]{1,0:T(8,128)(2,1)} copy(bf16[64,1280]{1,0:T(8,128)(2,1)S(1)} %get-tuple-element.92) | data formatting | bytes 327680

commit v3 on v2

--- a/solution.py
+++ b/solution.py
@@ -414,32 +414,81 @@
                 + w_tail[:, h : h + 1] * tail_out[:, hs]
             ).astype(BF16)
 
-    def z_copy(o):
+    def z_copy(source, slot, to):
         return pltpu.make_async_remote_copy(
-            src_ref=zsend.at[o - 1],
-            dst_ref=zrecv.at[o - 1],
-            send_sem=z_send_sem.at[o - 1],
-            recv_sem=z_recv_sem.at[o - 1],
-            device_id=(me, lax.rem(mk + o, nkv)),
+            src_ref=zsend.at[source],
+            dst_ref=zrecv.at[slot],
+            send_sem=z_send_sem.at[source],
+            recv_sem=z_recv_sem.at[slot],
+            device_id=(me, to),
             device_id_type=MESH,
         )
 
-    for o in range(1, nkv):
-        zsend[o - 1] = jnp.dot(
-            attn[...], wo[lax.rem(mk + o, nkv)], preferred_element_type=F32
-        ).astype(BF16)
-        z_copy(o).start()
-    acc = jnp.dot(attn[...], wo[mk], preferred_element_type=F32)
-    for o in range(1, nkv):
-        z_copy(o).wait_recv()
-        acc = acc + zrecv[o - 1].astype(F32)
-    out_ref[...] = acc.astype(BF16)
+    def partial(to):
+        return jnp.dot(attn[...], wo[to], preferred_element_type=F32)
+
+    if nkv == 4:
+        side = mk // 2
+        near_end = 3 * side
+        far_end = 3 - near_end
+        near = 1 + side
+        far = 2 - side
+        is_end = mk == near_end
+
+        @pl.when(is_end)
+        def _():
+            zsend[0] = partial(far_end).astype(BF16)
+            z_copy(0, 0, near).start()
+            zsend[1] = partial(far).astype(BF16)
+            z_copy(1, 1, far).start()
+            zsend[2] = partial(near).astype(BF16)
+            z_copy(2, 2, near).start()
+            acc = partial(mk)
+            z_copy(0, 2, near).wait_recv()
+            acc = acc + zrecv[2].astype(F32)
+            z_copy(1, 1, far).wait_recv()
+            out_ref[...] = (acc + zrecv[1].astype(F32)).astype(BF16)
+            z_copy(0, 0, near).wait_send()
+            z_copy(1, 1, far).wait_send()
+            z_copy(2, 2, near).wait_send()
+
+        @pl.when(jnp.logical_not(is_end))
+        def _():
+            zsend[1] = partial(far).astype(BF16)
+            z_copy(1, 3, far).start()
+            zsend[2] = partial(near_end).astype(BF16)
+            z_copy(2, 2, near_end).start()
+            onward = partial(far_end)
+            z_copy(0, 0, near_end).wait_recv()
+            zsend[0] = (onward + zrecv[0].astype(F32)).astype(BF16)
+            z_copy(0, 1, far_end).start()
+            acc = partial(mk)
+            z_copy(1, 3, far).wait_recv()
+            acc = acc + zrecv[3].astype(F32)
+            z_copy(2, 2, near_end).wait_recv()
+            acc = acc + zrecv[2].astype(F32)
+            z_copy(1, 1, far_end).wait_recv()
+            out_ref[...] = (acc + zrecv[1].astype(F32)).astype(BF16)
+            z_copy(0, 1, far_end).wait_send()
+            z_copy(1, 3, far).wait_send()
+            z_copy(2, 2, near_end).wait_send()
+
+    else:
+        for o in range(1, nkv):
+            to = lax.rem(mk + o, nkv)
+            zsend[o - 1] = partial(to).astype(BF16)
+            z_copy(o - 1, o - 1, to).start()
+        acc = partial(mk)
+        for o in range(1, nkv):
+            z_copy(o - 1, o - 1, lax.rem(mk + o, nkv)).wait_recv()
+            acc = acc + zrecv[o - 1].astype(F32)
+        out_ref[...] = acc.astype(BF16)
+        for o in range(1, nkv):
+            z_copy(o - 1, o - 1, lax.rem(mk + o, nkv)).wait_send()
     for o in range(1, n):
         q_copy(o).wait_send()
         for k in range(lkv):
             o_copy(k, o).wait_send()
-    for o in range(1, nkv):
-        z_copy(o).wait_send()
 
 
 def attend(cap, n, nkv, cid, *arrays):
@@ -484,7 +533,7 @@
             pltpu.VMEM((lkv, rows, HEAD_SIZE), F32),
             pltpu.VMEM((rows, qc), BF16),
             pltpu.VMEM((nkv - 1, rows, oc), BF16),
-            pltpu.VMEM((nkv - 1, rows, oc), BF16),
+            pltpu.VMEM((nkv, rows, oc), BF16),
             dma,
             dma((QUERY_PER_KEY + 2,)),
             dma((nkv,)),
@@ -497,7 +546,7 @@
             dma((lkv, n)),
             dma((lkv, n)),
             dma((nkv - 1,)),
-            dma((nkv - 1,)),
+            dma((nkv,)),
         ],
         compiler_params=pltpu.CompilerParams(
             collective_id=cid, has_side_effects=True, vmem_limit_bytes=62 * 1024 * 1024

time: 55.9 us -> 55.4 us (level)
  the two profiles are of different devices: /device:TPU:9 before, /device:TPU:0 now
where the time goes in v3:
time: 55.4 us; the launch traced here: 55.2 us
  Pallas kernels  52 us (94%)
  other arithmetic  1.46 us (3%)
  local copies, waits for them, and re-layouts  0.67 us (1%)
  between operations  0.67 us (1%)
    pallas_call x1, Pallas kernels, attend(): pl.pallas_call(functools.partial(body, cap, n, nkv), out_shape=jax.ShapeD...  52 us

profile of v3, /device:TPU:0, one launch (start us, length us, event | category | flops | bytes accessed | tf_op | source)
XLA Modules:
  0.0 55.2 jit_solution(10817164021046657020)
XLA Ops:
  0.0 0.7 %fusion = s32[512]{0:T(512)S(1)} fusion(s32[512]{0:T(512)} %param.26, s32[512]{0:T(512)} %param.27), kind=kLoop, calls=%fused_computation.7 | loop fusion | flops 12800 | bytes 6144 | tf_op jit(solution)/shard_map/add | solution.py:597
  0.7 0.1 convert_reduce_fusion
  0.8 0.6 %reduce_max.9 = s32[]{:T(128)} reduce(s32[64]{0:T(128)S(1)} %convert_reduce_fusion, s32[]{:T(128)} %constant.26.clone.1), dimensions={0}, to_apply=%region_1.2 | reduce | flops 63 | bytes 264 | tf_op jit(solution)/shard_map/reduce_max | solution.py:602
  2.1 52.4 %conditional.1 = (bf16[64,1280]{1,0:T(8,128)(2,1)S(1)}) conditional(s32[]{:T(128)} %convert_element_type.7, (bf16[5120]{0:T(1024)(128)(2,1)}, s32[512]{0:T(512)}, s32[512]{0:T(512)}, s32[48]{0:T(128)}, s32[64]{0:T(128)}, /*index=5*/bf16[64,5120]{1,0:T(8,128)(2,1)}, bf16[5120,1280]{1,0:T(8,128)(2,1)}, bf16[5120,256]{1,0:T(8,128)(2,1)}, ...), branch_computations={%region_2.3_spmd, %region_3.4_spmd} | conditional | bytes 8 | solution.py:601
  2.3 52.0 %attend32.1 = bf16[64,1280]{1,0:T(8,128)(2,1)S(1)} custom-call(bf16[5120]{0:T(1024)(128)(2,1)} %get-tuple-element.122.gain_ref, s32[1,512]{1,0:T(1,128)} %bitcast.19, s32[1,512]{1,0:T(1,128)} %bitcast.17, s32[1,48]{1,0:T(1,128)} %bitcast.21, s32[1,64]{1,0:T(1,128)} %bitcast.23, bf16[64,5120]{1,0:T(8,128)(2,1)} %get-tuple-element.128.hidden_hbm, ...), custom_call_target="tpu_custom_call" | custom-call | tf_op jit(solution)/shard_map/cond/branch_1_fun/attend32/pallas_call | solution.py:507
  54.5 0.7 %copy.44 = bf16[64,1280]{1,0:T(8,128)(2,1)} copy(bf16[64,1280]{1,0:T(8,128)(2,1)S(1)} %get-tuple-element.92) | data formatting | bytes 327680
